TPU v7x, 32 devices: a whole 2x2x4 slice. The times are simulated.
32 devices in a mesh: seq: 16 (over z, y, core), tp: 2 (over x).
Axes of the slice: x: 2, y: 2, z: 4, core: 2. Of those that a mesh axis runs over, the one named last changes fastest.
Arguments:
- queries: bfloat16 [4096, 8, 8, 128], P('seq', None, 'tp'), may hold values from -6 to 6
- keys: bfloat16 [4096, 8, 128], P('seq'), may hold values from -6 to 6
- values: bfloat16 [4096, 8, 128], P('seq'), may hold values from -6 to 6
- grad_out: bfloat16 [4096, 8, 8, 128], P('seq', None, 'tp'), may hold values from -6 to 6
- exponents: int32 [32, 8, 8], P('seq', None, 'tp'), may hold values from -2 to 2
- lengths: int32 [32], replicated, may hold values from 1 to 256, 4096 in all
Outputs:
- grad_queries: bfloat16 [4096, 8, 8, 128], P('seq', None, 'tp')
- grad_keys: bfloat16 [4096, 8, 128], P('seq', 'tp')
- grad_values: bfloat16 [4096, 8, 128], P('seq', 'tp')
Inputs may be any that keep to these rules, and one draw needn't show every extreme that they name: No document has more than 256 tokens (at least one has exactly 256); the lengths sum to 4096. `exponents`: one exponent for each block of 128 tokens of one query head.
All inputs are finite; a program needn't handle non-finite values.
Results may differ from a plain program's by a relative error of at most 0.03.
Values may be sent and summed in bfloat16 or wider, within the bound.
A program may use at most 64 MiB of HBM per device.

v0:
```python
import jax
import jax.numpy as jnp
from jax import lax
from jax.sharding import PartitionSpec as P


def passed_along(block, axis, distance):
    devices = range(lax.axis_size(axis))
    route = [(i - distance, i) for i in devices if i - distance in devices]
    return lax.ppermute(block, axis, route)


def window_docs(lengths, first_row, count):
    positions = first_row + jnp.arange(count, dtype=jnp.int32)
    doc_ends = jnp.cumsum(lengths)
    return (positions, jnp.sum((doc_ends[None, :] <= positions[:, None]).astype(jnp.int32), axis=1))


def group_grads(query_grp, dout_grp, key_window, value_window, allowed, scaling):
    scores = (
        jnp.einsum("qrd,kd->rqk", query_grp, key_window, preferred_element_type=jnp.float32)
        * scaling
    )
    scores = jnp.where(allowed[None], scores, -1e30)
    row_max = jnp.max(scores, axis=-1, keepdims=True)
    shifted = jnp.exp(scores - row_max)
    row_sum = jnp.sum(shifted, axis=-1, keepdims=True)
    attn_w = shifted / row_sum
    attn_low = attn_w.astype(jnp.bfloat16)
    attn_out = jnp.einsum(
        "rqk,kd->qrd", attn_low, value_window, preferred_element_type=jnp.float32
    ).astype(jnp.bfloat16)
    row_delta = jnp.transpose(
        jnp.sum(dout_grp.astype(jnp.float32) * attn_out.astype(jnp.float32), axis=-1)
    )[..., None]
    grad_probs = jnp.einsum(
        "qrd,kd->rqk", dout_grp, value_window, preferred_element_type=jnp.float32
    )
    grad_low = (scaling * attn_w * (grad_probs - row_delta)).astype(jnp.bfloat16)
    grad_query = jnp.einsum(
        "rqk,kd->qrd", grad_low, key_window, preferred_element_type=jnp.float32
    ).astype(jnp.bfloat16)
    return (attn_low, grad_low, grad_query, row_max[..., 0], row_sum[..., 0], row_delta[..., 0])


def core_grads(queries, scaled, keys, values, lengths, scaling):
    row_count = queries.shape[0]
    first_row = lax.axis_index("seq") * row_count
    earlier_keys, earlier_values = passed_along((keys, values), "seq", 1)
    key_window = jnp.moveaxis(jnp.concatenate([earlier_keys, keys], axis=0), 1, 0)
    value_window = jnp.moveaxis(jnp.concatenate([earlier_values, values], axis=0), 1, 0)
    query_pos, query_doc = window_docs(lengths, first_row, row_count)
    key_pos, key_doc = window_docs(lengths, first_row - row_count, 2 * row_count)
    allowed = (
        (query_doc[:, None] == key_doc[None, :])
        & (key_pos[None, :] <= query_pos[:, None])
        & (key_pos[None, :] >= 0)
    )
    query_major = jnp.moveaxis(queries, 1, 0)
    dout_major = jnp.moveaxis(scaled, 1, 0)

    def full_group(inputs):
        query_grp, dout_grp, key_grp, value_grp = inputs
        attn_low, grad_low, grad_query, row_max, row_sum, row_delta = group_grads(
            query_grp, dout_grp, key_grp, value_grp, allowed, scaling
        )
        grad_key = jnp.einsum(
            "rqk,qrd->kd", grad_low, query_grp, preferred_element_type=jnp.float32
        )
        grad_value = jnp.einsum(
            "rqk,qrd->kd", attn_low, dout_grp, preferred_element_type=jnp.float32
        )
        return (grad_query, grad_key, grad_value)

    grad_query, key_terms, value_terms = lax.map(
        full_group, (query_major, dout_major, key_window, value_window)
    )
    back_keys, back_values = (
        passed_along(key_terms[:, :row_count].astype(jnp.bfloat16), "seq", -1).astype(jnp.float32),
        passed_along(value_terms[:, :row_count].astype(jnp.bfloat16), "seq", -1).astype(
            jnp.float32
        ),
    )
    key_total = key_terms[:, row_count:] + back_keys
    value_total = value_terms[:, row_count:] + back_values
    return (grad_query, key_total, value_total)


def per_device(queries, keys, values, grad_out, exponents, lengths):
    row_count, groups, local_heads, head_width = queries.shape
    scaling = head_width ** (-0.5)
    exp_block = row_count // exponents.shape[0]
    factor = jnp.exp2(exponents.astype(jnp.float32)).astype(jnp.bfloat16)
    scaled = (
        grad_out.reshape(row_count // exp_block, exp_block, groups, local_heads, head_width)
        * factor[:, None, :, :, None]
    )
    scaled = scaled.reshape(row_count, groups, local_heads, head_width)
    grad_query, key_total, value_total = core_grads(queries, scaled, keys, values, lengths, scaling)
    summed_keys, summed_values = (
        lax.psum_scatter(key_total, "tp", scatter_dimension=0, tiled=True),
        lax.psum_scatter(value_total, "tp", scatter_dimension=0, tiled=True),
    )
    grad_queries = jnp.moveaxis(grad_query, 0, 1)
    grad_keys = jnp.moveaxis(summed_keys, 0, 1).astype(jnp.bfloat16)
    grad_values = jnp.moveaxis(summed_values, 0, 1).astype(jnp.bfloat16)
    return (grad_queries, grad_keys, grad_values)


def solution(mesh):
    placed = (
        P("seq", None, "tp", None),
        P("seq", None, None),
        P("seq", None, None),
        P("seq", None, "tp", None),
        P("seq", None, "tp"),
        P(),
    )
    return jax.shard_map(
        per_device,
        mesh=mesh,
        in_specs=placed,
        out_specs=(P("seq", None, "tp", None), P("seq", "tp", None), P("seq", "tp", None)),
        check_vma=False,
    )
```

profile of v0, /device:TPU:1, one launch (start us, length us, event | category | flops | bytes accessed | tf_op | source)
XLA Modules:
  0.0 202.5 jit_solution(10995476012953416616)
XLA Ops:
  8.3 4.5 %collective-permute-start.1 = (bf16[256,8,128]{2,0,1:T(8,128)(2,1)S(1)}, bf16[256,8,128]{2,0,1:T(8,128)(2,1)}, u32[]{:S(2)}, u32[]{:S(2)}) collective-permute-start(bf16[256,8,128]{2,0,1:T(8,128)(2,1)S(1)} %copy.69), channel_id=1, source_target_pairs={{0,2},{2,4},{4,6},{6,8},{8,10},{10,12},{12,14},{14,16},{16,18},{18... | collective-permute-start | bytes 1572872 | tf_op jit(solution)/shard_map/ppermute | solution.py:10
  16.8 2.6 %copy.90 = bf16[256,8,4,128]{3,0,2,1:T(8,128)(2,1)S(1)} copy(bf16[256,8,4,128]{3,2,1,0:T(4,128)(2,1)} %param.8) | data formatting | bytes 4194304 | tf_op args[0]
  19.3 2.9 %fusion.74 = bf16[8,256,4,128]{3,1,2,0:T(8,128)(2,1)} fusion(bf16[256,8,4,128]{3,2,1,0:T(4,128)(2,1)S(1)} %copy-done.2, bf16[256,8,4]{0,2,1:T(4,128)(2,1)S(1)} %mul.33), kind=kLoop, calls=%fused_computation.55 | loop fusion | flops 1048576 | bytes 4210688 | tf_op jit(solution)/shard_map/transpose | solution.py:60
  25.7 109.1 %while.15 = (s32[]{:T(128)}, bf16[8,256,4,128]{3,2,0,1:T(4,128)(2,1)}, f32[8,512,128]{2,1,0:T(8,128)}, f32[8,512,128]{2,1,0:T(8,128)}, bf16[8,512,128]{2,1,0:T(8...) while((s32[]{:T(128)}, ...), condition=%wide.region_7.8_spmd.clone, body=%wide.region_3.7_spmd.clone.sunk | while | flops 1085016576 | bytes 29136588 | solution.py:75
  28.3 2.5 %fusion.121 = f32[256,4]{0,1:T(4,128)S(1)} fusion(bf16[8,256,4,128]{3,1,2,0:T(8,128)(2,1)} %get-tuple-element.240, s32[]{:T(128)S(6)} %copy.100, bf16[8,512,128]{2,1,0:T(8,128)(2,1)} %get-tuple-element.239, f32[4,256]{1,0:T(4,128)S(1)} %get-tuple-element.203, pred[256,512]{0,1:T(8,128)(4,1)S(1)} %and_and_fusion.2, ...), kind=kOutput, calls=%fused_computation.13.clone.1 | convolution fusion | flops 271712768 | bytes 927744 | tf_op jit(solution)/shard_map/while/body/eval_jaxpr/rqk,kd->qrd/dot_general | solution.py:30
  36.4 3.0 %fusion.125 = f32[8,512,128]{2,1,0:T(8,128)} fusion(f32[8,512,128]{2,1,0:T(8,128)} %get-tuple-element.222, s32[]{:T(128)S(6)} %copy.100, bf16[8,256,4,128]{3,1,2,0:T(8,128)(2,1)} %get-tuple-element.240, f32[4,256]{1,0:T(4,128)S(1)} %get-tuple-element.203, pred[256,512]{0,1:T(8,128)(4,1)S(1)} %and_and_fusion.2, bf16[8,256,4,128]{3,1,2,0:T(8,128)(2,1)} %copy-done, ...), kind=kOutput, calls=%fused_computation.16.clone.1 | convolution fusion | flops 271058432 | bytes 1054720 | tf_op jit(solution)/shard_map/while/body/eval_jaxpr/rqk,qrd->kd/dot_general | solution.py:70
  41.9 2.5 %fusion.121 = f32[256,4]{0,1:T(4,128)S(1)} fusion(bf16[8,256,4,128]{3,1,2,0:T(8,128)(2,1)} %get-tuple-element.240, s32[]{:T(128)S(6)} %copy.100, bf16[8,512,128]{2,1,0:T(8,128)(2,1)} %get-tuple-element.239, f32[4,256]{1,0:T(4,128)S(1)} %get-tuple-element.203, pred[256,512]{0,1:T(8,128)(4,1)S(1)} %and_and_fusion.2, ...), kind=kOutput, calls=%fused_computation.13.clone.1 | convolution fusion | flops 271712768 | bytes 927744 | tf_op jit(solution)/shard_map/while/body/eval_jaxpr/rqk,kd->qrd/dot_general | solution.py:30
  50.0 3.0 %fusion.125 = f32[8,512,128]{2,1,0:T(8,128)} fusion(f32[8,512,128]{2,1,0:T(8,128)} %get-tuple-element.222, s32[]{:T(128)S(6)} %copy.100, bf16[8,256,4,128]{3,1,2,0:T(8,128)(2,1)} %get-tuple-element.240, f32[4,256]{1,0:T(4,128)S(1)} %get-tuple-element.203, pred[256,512]{0,1:T(8,128)(4,1)S(1)} %and_and_fusion.2, bf16[8,256,4,128]{3,1,2,0:T(8,128)(2,1)} %copy-done, ...), kind=kOutput, calls=%fused_computation.16.clone.1 | convolution fusion | flops 271058432 | bytes 1054720 | tf_op jit(solution)/shard_map/while/body/eval_jaxpr/rqk,qrd->kd/dot_general | solution.py:70
  55.5 2.5 %fusion.121 = f32[256,4]{0,1:T(4,128)S(1)} fusion(bf16[8,256,4,128]{3,1,2,0:T(8,128)(2,1)} %get-tuple-element.240, s32[]{:T(128)S(6)} %copy.100, bf16[8,512,128]{2,1,0:T(8,128)(2,1)} %get-tuple-element.239, f32[4,256]{1,0:T(4,128)S(1)} %get-tuple-element.203, pred[256,512]{0,1:T(8,128)(4,1)S(1)} %and_and_fusion.2, ...), kind=kOutput, calls=%fused_computation.13.clone.1 | convolution fusion | flops 271712768 | bytes 927744 | tf_op jit(solution)/shard_map/while/body/eval_jaxpr/rqk,kd->qrd/dot_general | solution.py:30
  63.6 3.0 %fusion.125 = f32[8,512,128]{2,1,0:T(8,128)} fusion(f32[8,512,128]{2,1,0:T(8,128)} %get-tuple-element.222, s32[]{:T(128)S(6)} %copy.100, bf16[8,256,4,128]{3,1,2,0:T(8,128)(2,1)} %get-tuple-element.240, f32[4,256]{1,0:T(4,128)S(1)} %get-tuple-element.203, pred[256,512]{0,1:T(8,128)(4,1)S(1)} %and_and_fusion.2, bf16[8,256,4,128]{3,1,2,0:T(8,128)(2,1)} %copy-done, ...), kind=kOutput, calls=%fused_computation.16.clone.1 | convolution fusion | flops 271058432 | bytes 1054720 | tf_op jit(solution)/shard_map/while/body/eval_jaxpr/rqk,qrd->kd/dot_general | solution.py:70
  69.1 2.5 %fusion.121 = f32[256,4]{0,1:T(4,128)S(1)} fusion(bf16[8,256,4,128]{3,1,2,0:T(8,128)(2,1)} %get-tuple-element.240, s32[]{:T(128)S(6)} %copy.100, bf16[8,512,128]{2,1,0:T(8,128)(2,1)} %get-tuple-element.239, f32[4,256]{1,0:T(4,128)S(1)} %get-tuple-element.203, pred[256,512]{0,1:T(8,128)(4,1)S(1)} %and_and_fusion.2, ...), kind=kOutput, calls=%fused_computation.13.clone.1 | convolution fusion | flops 271712768 | bytes 927744 | tf_op jit(solution)/shard_map/while/body/eval_jaxpr/rqk,kd->qrd/dot_general | solution.py:30
  77.3 3.0 %fusion.125 = f32[8,512,128]{2,1,0:T(8,128)} fusion(f32[8,512,128]{2,1,0:T(8,128)} %get-tuple-element.222, s32[]{:T(128)S(6)} %copy.100, bf16[8,256,4,128]{3,1,2,0:T(8,128)(2,1)} %get-tuple-element.240, f32[4,256]{1,0:T(4,128)S(1)} %get-tuple-element.203, pred[256,512]{0,1:T(8,128)(4,1)S(1)} %and_and_fusion.2, bf16[8,256,4,128]{3,1,2,0:T(8,128)(2,1)} %copy-done, ...), kind=kOutput, calls=%fused_computation.16.clone.1 | convolution fusion | flops 271058432 | bytes 1054720 | tf_op jit(solution)/shard_map/while/body/eval_jaxpr/rqk,qrd->kd/dot_general | solution.py:70
  90.9 3.0 %fusion.125 = f32[8,512,128]{2,1,0:T(8,128)} fusion(f32[8,512,128]{2,1,0:T(8,128)} %get-tuple-element.222, s32[]{:T(128)S(6)} %copy.100, bf16[8,256,4,128]{3,1,2,0:T(8,128)(2,1)} %get-tuple-element.240, f32[4,256]{1,0:T(4,128)S(1)} %get-tuple-element.203, pred[256,512]{0,1:T(8,128)(4,1)S(1)} %and_and_fusion.2, bf16[8,256,4,128]{3,1,2,0:T(8,128)(2,1)} %copy-done, ...), kind=kOutput, calls=%fused_computation.16.clone.1 | convolution fusion | flops 271058432 | bytes 1054720 | tf_op jit(solution)/shard_map/while/body/eval_jaxpr/rqk,qrd->kd/dot_general | solution.py:70
  96.4 2.5 %fusion.121 = f32[256,4]{0,1:T(4,128)S(1)} fusion(bf16[8,256,4,128]{3,1,2,0:T(8,128)(2,1)} %get-tuple-element.240, s32[]{:T(128)S(6)} %copy.100, bf16[8,512,128]{2,1,0:T(8,128)(2,1)} %get-tuple-element.239, f32[4,256]{1,0:T(4,128)S(1)} %get-tuple-element.203, pred[256,512]{0,1:T(8,128)(4,1)S(1)} %and_and_fusion.2, ...), kind=kOutput, calls=%fused_computation.13.clone.1 | convolution fusion | flops 271712768 | bytes 927744 | tf_op jit(solution)/shard_map/while/body/eval_jaxpr/rqk,kd->qrd/dot_general | solution.py:30
  104.6 3.0 %fusion.125 = f32[8,512,128]{2,1,0:T(8,128)} fusion(f32[8,512,128]{2,1,0:T(8,128)} %get-tuple-element.222, s32[]{:T(128)S(6)} %copy.100, bf16[8,256,4,128]{3,1,2,0:T(8,128)(2,1)} %get-tuple-element.240, f32[4,256]{1,0:T(4,128)S(1)} %get-tuple-element.203, pred[256,512]{0,1:T(8,128)(4,1)S(1)} %and_and_fusion.2, bf16[8,256,4,128]{3,1,2,0:T(8,128)(2,1)} %copy-done, ...), kind=kOutput, calls=%fused_computation.16.clone.1 | convolution fusion | flops 271058432 | bytes 1054720 | tf_op jit(solution)/shard_map/while/body/eval_jaxpr/rqk,qrd->kd/dot_general | solution.py:70
  110.1 2.5 %fusion.121 = f32[256,4]{0,1:T(4,128)S(1)} fusion(bf16[8,256,4,128]{3,1,2,0:T(8,128)(2,1)} %get-tuple-element.240, s32[]{:T(128)S(6)} %copy.100, bf16[8,512,128]{2,1,0:T(8,128)(2,1)} %get-tuple-element.239, f32[4,256]{1,0:T(4,128)S(1)} %get-tuple-element.203, pred[256,512]{0,1:T(8,128)(4,1)S(1)} %and_and_fusion.2, ...), kind=kOutput, calls=%fused_computation.13.clone.1 | convolution fusion | flops 271712768 | bytes 927744 | tf_op jit(solution)/shard_map/while/body/eval_jaxpr/rqk,kd->qrd/dot_general | solution.py:30
  118.2 3.0 %fusion.125 = f32[8,512,128]{2,1,0:T(8,128)} fusion(f32[8,512,128]{2,1,0:T(8,128)} %get-tuple-element.222, s32[]{:T(128)S(6)} %copy.100, bf16[8,256,4,128]{3,1,2,0:T(8,128)(2,1)} %get-tuple-element.240, f32[4,256]{1,0:T(4,128)S(1)} %get-tuple-element.203, pred[256,512]{0,1:T(8,128)(4,1)S(1)} %and_and_fusion.2, bf16[8,256,4,128]{3,1,2,0:T(8,128)(2,1)} %copy-done, ...), kind=kOutput, calls=%fused_computation.16.clone.1 | convolution fusion | flops 271058432 | bytes 1054720 | tf_op jit(solution)/shard_map/while/body/eval_jaxpr/rqk,qrd->kd/dot_general | solution.py:70
  123.7 2.5 %fusion.121 = f32[256,4]{0,1:T(4,128)S(1)} fusion(bf16[8,256,4,128]{3,1,2,0:T(8,128)(2,1)} %get-tuple-element.240, s32[]{:T(128)S(6)} %copy.100, bf16[8,512,128]{2,1,0:T(8,128)(2,1)} %get-tuple-element.239, f32[4,256]{1,0:T(4,128)S(1)} %get-tuple-element.203, pred[256,512]{0,1:T(8,128)(4,1)S(1)} %and_and_fusion.2, ...), kind=kOutput, calls=%fused_computation.13.clone.1 | convolution fusion | flops 271712768 | bytes 927744 | tf_op jit(solution)/shard_map/while/body/eval_jaxpr/rqk,kd->qrd/dot_general | solution.py:30
  131.8 3.0 %fusion.125 = f32[8,512,128]{2,1,0:T(8,128)} fusion(f32[8,512,128]{2,1,0:T(8,128)} %get-tuple-element.222, s32[]{:T(128)S(6)} %copy.100, bf16[8,256,4,128]{3,1,2,0:T(8,128)(2,1)} %get-tuple-element.240, f32[4,256]{1,0:T(4,128)S(1)} %get-tuple-element.203, pred[256,512]{0,1:T(8,128)(4,1)S(1)} %and_and_fusion.2, bf16[8,256,4,128]{3,1,2,0:T(8,128)(2,1)} %copy-done, ...), kind=kOutput, calls=%fused_computation.16.clone.1 | convolution fusion | flops 271058432 | bytes 1054720 | tf_op jit(solution)/shard_map/while/body/eval_jaxpr/rqk,qrd->kd/dot_general | solution.py:70
  136.1 3.1 %collective-permute-start.2 = (bf16[8,256,128]{2,1,0:T(8,128)(2,1)S(1)}, bf16[8,256,128]{2,1,0:T(8,128)(2,1)S(1)}, u32[]{:S(2)}, u32[]{:S(2)}) collective-permute-start(bf16[8,256,128]{2,1,0:T(8,128)(2,1)S(1)} %slice.25), channel_id=1, source_target_pairs={{2,0},{4,2},{6,4},{8,6},{10,8},{12,10},{14,12},{16,14},{18,16},{20... | collective-permute-start | bytes 1572872 | tf_op jit(solution)/shard_map/ppermute | solution.py:10
  139.3 8.4 %collective-permute-done.2 = bf16[8,256,128]{2,1,0:T(8,128)(2,1)S(1)} collective-permute-done((bf16[8,256,128]{2,1,0:T(8,128)(2,1)S(1)}, bf16[8,256,128]{2,1,0:T(8,128)(2,1)S(1)}, u32[]{:S(2)}, u32[]{:S(2)}) %collective-permute-start.2) | collective-permute-done | bytes 524320 | tf_op jit(solution)/shard_map/ppermute | solution.py:10
  152.0 9.0 %collective-permute-done.3 = bf16[8,256,128]{2,1,0:T(8,128)(2,1)S(1)} collective-permute-done((bf16[8,256,128]{2,1,0:T(8,128)(2,1)S(1)}, bf16[8,256,128]{2,1,0:T(8,128)(2,1)S(1)}, u32[]{:S(2)}, u32[]{:S(2)}) %collective-permute-start.3) | collective-permute-done | bytes 524320 | tf_op jit(solution)/shard_map/ppermute | solution.py:10
  162.2 8.9 %reduce-scatter.3.cloned.1.call-done = f32[4,256,128]{2,1,0:T(8,128)} async-done(((f32[8,256,128]{2,1,0:T(8,128)}), f32[4,256,128]{2,1,0:T(8,128)}) %reduce-scatter.3.cloned.1.call-update) | async-done | bytes 524304 | tf_op jit(solution)/shard_map/reduce_scatter | solution.py:101
  173.0 20.7 %reduce-scatter.5.cloned.1.call-done = f32[4,256,128]{2,1,0:T(8,128)} async-done(((f32[8,256,128]{2,1,0:T(8,128)}), f32[4,256,128]{2,1,0:T(8,128)}) %reduce-scatter.5.cloned.1.call-update) | async-done | bytes 524304 | tf_op jit(solution)/shard_map/reduce_scatter | solution.py:102
  (136 shorter events, 86.8 us)
Async XLA Ops:
  7.2 8.8 %copy-start.6 = (s32[2,8,4]{1,2,0:T(4,128)S(1)}, s32[2,8,4]{1,2,0:T(4,128)}, u32[]{:S(2)}) copy-start(s32[2,8,4]{1,2,0:T(4,128)} %param.12) | copy-start | bytes 772
  7.2 8.8 %copy-start.7 = (s32[32]{0:T(128)S(1)}, s32[32]{0:T(128)}, u32[]{:S(2)}) copy-start(s32[32]{0:T(128)} %param.13) | copy-start | bytes 388
  7.2 163.8 %reduce-scatter.3.cloned.1.call-start = ((), (), s32[]{:S(2)}) async-start(), calls=%async_computation.2 | async-start | bytes 1572864 | tf_op jit(solution)/shard_map/reduce_scatter | solution.py:101
  8.3 13.9 %collective-permute-start.1 = (bf16[256,8,128]{2,0,1:T(8,128)(2,1)S(1)}, bf16[256,8,128]{2,0,1:T(8,128)(2,1)}, u32[]{:S(2)}, u32[]{:S(2)}) collective-permute-start(bf16[256,8,128]{2,0,1:T(8,128)(2,1)S(1)} %copy.69), channel_id=1, source_target_pairs={{0,2},{2,4},{4,6},{6,8},{8,10},{10,12},{12,14},{14,16},{16,18},{18... | collective-permute-start | bytes 1572872 | tf_op jit(solution)/shard_map/ppermute | solution.py:10
  14.0 5.3 %copy-start.3 = (bf16[256,8,128]{2,0,1:T(8,128)(2,1)}, bf16[256,8,128]{2,0,1:T(8,128)(2,1)S(1)}, u32[]{:S(2)}) copy-start(bf16[256,8,128]{2,0,1:T(8,128)(2,1)S(1)} %copy.66) | copy-start | bytes 1572868
  14.0 10.6 %collective-permute-start = (bf16[256,8,128]{2,0,1:T(8,128)(2,1)S(1)}, bf16[256,8,128]{2,0,1:T(8,128)(2,1)}, u32[]{:S(2)}, u32[]{:S(2)}) collective-permute-start(bf16[256,8,128]{2,0,1:T(8,128)(2,1)S(1)} %copy.66), channel_id=1, source_target_pairs={{0,2},{2,4},{4,6},{6,8},{8,10},{10,12},{12,14},{14,16},{16,18},{18... | collective-permute-start | bytes 1572872 | tf_op jit(solution)/shard_map/ppermute | solution.py:10
  25.7 5.0 %copy-start = (bf16[8,256,4,128]{3,1,2,0:T(8,128)(2,1)}, bf16[8,256,4,128]{3,1,2,0:T(8,128)(2,1)S(1)}, u32[]{:S(2)}) copy-start(bf16[8,256,4,128]{3,1,2,0:T(8,128)(2,1)S(1)} %get-tuple-element.238) | copy-start | bytes 6291460 | tf_op jit(solution)/shard_map/while
  39.4 5.0 %copy-start = (bf16[8,256,4,128]{3,1,2,0:T(8,128)(2,1)}, bf16[8,256,4,128]{3,1,2,0:T(8,128)(2,1)S(1)}, u32[]{:S(2)}) copy-start(bf16[8,256,4,128]{3,1,2,0:T(8,128)(2,1)S(1)} %get-tuple-element.238) | copy-start | bytes 6291460 | tf_op jit(solution)/shard_map/while
  53.0 5.0 %copy-start = (bf16[8,256,4,128]{3,1,2,0:T(8,128)(2,1)}, bf16[8,256,4,128]{3,1,2,0:T(8,128)(2,1)S(1)}, u32[]{:S(2)}) copy-start(bf16[8,256,4,128]{3,1,2,0:T(8,128)(2,1)S(1)} %get-tuple-element.238) | copy-start | bytes 6291460 | tf_op jit(solution)/shard_map/while
  63.6 3.0 %copy-start.1 = (bf16[8,256,4,128]{3,1,2,0:T(8,128)(2,1)S(1)}, bf16[8,256,4,128]{3,1,2,0:T(8,128)(2,1)}, u32[]{:S(2)}) copy-start(bf16[8,256,4,128]{3,1,2,0:T(8,128)(2,1)} %copy-done) | copy-start | bytes 6291460 | tf_op jit(solution)/shard_map/while
  66.6 5.0 %copy-start = (bf16[8,256,4,128]{3,1,2,0:T(8,128)(2,1)}, bf16[8,256,4,128]{3,1,2,0:T(8,128)(2,1)S(1)}, u32[]{:S(2)}) copy-start(bf16[8,256,4,128]{3,1,2,0:T(8,128)(2,1)S(1)} %get-tuple-element.238) | copy-start | bytes 6291460 | tf_op jit(solution)/shard_map/while
  77.3 3.0 %copy-start.1 = (bf16[8,256,4,128]{3,1,2,0:T(8,128)(2,1)S(1)}, bf16[8,256,4,128]{3,1,2,0:T(8,128)(2,1)}, u32[]{:S(2)}) copy-start(bf16[8,256,4,128]{3,1,2,0:T(8,128)(2,1)} %copy-done) | copy-start | bytes 6291460 | tf_op jit(solution)/shard_map/while
  80.3 5.0 %copy-start = (bf16[8,256,4,128]{3,1,2,0:T(8,128)(2,1)}, bf16[8,256,4,128]{3,1,2,0:T(8,128)(2,1)S(1)}, u32[]{:S(2)}) copy-start(bf16[8,256,4,128]{3,1,2,0:T(8,128)(2,1)S(1)} %get-tuple-element.238) | copy-start | bytes 6291460 | tf_op jit(solution)/shard_map/while
  90.9 3.0 %copy-start.1 = (bf16[8,256,4,128]{3,1,2,0:T(8,128)(2,1)S(1)}, bf16[8,256,4,128]{3,1,2,0:T(8,128)(2,1)}, u32[]{:S(2)}) copy-start(bf16[8,256,4,128]{3,1,2,0:T(8,128)(2,1)} %copy-done) | copy-start | bytes 6291460 | tf_op jit(solution)/shard_map/while
  93.9 5.0 %copy-start = (bf16[8,256,4,128]{3,1,2,0:T(8,128)(2,1)}, bf16[8,256,4,128]{3,1,2,0:T(8,128)(2,1)S(1)}, u32[]{:S(2)}) copy-start(bf16[8,256,4,128]{3,1,2,0:T(8,128)(2,1)S(1)} %get-tuple-element.238) | copy-start | bytes 6291460 | tf_op jit(solution)/shard_map/while
  104.6 3.0 %copy-start.1 = (bf16[8,256,4,128]{3,1,2,0:T(8,128)(2,1)S(1)}, bf16[8,256,4,128]{3,1,2,0:T(8,128)(2,1)}, u32[]{:S(2)}) copy-start(bf16[8,256,4,128]{3,1,2,0:T(8,128)(2,1)} %copy-done) | copy-start | bytes 6291460 | tf_op jit(solution)/shard_map/while
  107.6 5.0 %copy-start = (bf16[8,256,4,128]{3,1,2,0:T(8,128)(2,1)}, bf16[8,256,4,128]{3,1,2,0:T(8,128)(2,1)S(1)}, u32[]{:S(2)}) copy-start(bf16[8,256,4,128]{3,1,2,0:T(8,128)(2,1)S(1)} %get-tuple-element.238) | copy-start | bytes 6291460 | tf_op jit(solution)/shard_map/while
  118.2 3.0 %copy-start.1 = (bf16[8,256,4,128]{3,1,2,0:T(8,128)(2,1)S(1)}, bf16[8,256,4,128]{3,1,2,0:T(8,128)(2,1)}, u32[]{:S(2)}) copy-start(bf16[8,256,4,128]{3,1,2,0:T(8,128)(2,1)} %copy-done) | copy-start | bytes 6291460 | tf_op jit(solution)/shard_map/while
  121.2 5.0 %copy-start = (bf16[8,256,4,128]{3,1,2,0:T(8,128)(2,1)}, bf16[8,256,4,128]{3,1,2,0:T(8,128)(2,1)S(1)}, u32[]{:S(2)}) copy-start(bf16[8,256,4,128]{3,1,2,0:T(8,128)(2,1)S(1)} %get-tuple-element.238) | copy-start | bytes 6291460 | tf_op jit(solution)/shard_map/while
  131.8 3.0 %copy-start.1 = (bf16[8,256,4,128]{3,1,2,0:T(8,128)(2,1)S(1)}, bf16[8,256,4,128]{3,1,2,0:T(8,128)(2,1)}, u32[]{:S(2)}) copy-start(bf16[8,256,4,128]{3,1,2,0:T(8,128)(2,1)} %copy-done) | copy-start | bytes 6291460 | tf_op jit(solution)/shard_map/while
  136.1 13.9 %copy-start.5 = (f32[8,512,128]{2,1,0:T(8,128)S(1)}, f32[8,512,128]{2,1,0:T(8,128)}, u32[]{:S(2)}) copy-start(f32[8,512,128]{2,1,0:T(8,128)} %get-tuple-element.54) | copy-start | bytes 6291460
  136.1 11.5 %collective-permute-start.2 = (bf16[8,256,128]{2,1,0:T(8,128)(2,1)S(1)}, bf16[8,256,128]{2,1,0:T(8,128)(2,1)S(1)}, u32[]{:S(2)}, u32[]{:S(2)}) collective-permute-start(bf16[8,256,128]{2,1,0:T(8,128)(2,1)S(1)} %slice.25), channel_id=1, source_target_pairs={{2,0},{4,2},{6,4},{8,6},{10,8},{12,10},{14,12},{16,14},{18,16},{20... | collective-permute-start | bytes 1572872 | tf_op jit(solution)/shard_map/ppermute | solution.py:10
  150.0 43.7 %reduce-scatter.5.cloned.1.call-start = ((), (), s32[]{:S(2)}) async-start(), calls=%async_computation.3 | async-start | bytes 1572864 | tf_op jit(solution)/shard_map/reduce_scatter | solution.py:102
  150.1 10.9 %collective-permute-start.3 = (bf16[8,256,128]{2,1,0:T(8,128)(2,1)S(1)}, bf16[8,256,128]{2,1,0:T(8,128)(2,1)S(1)}, u32[]{:S(2)}, u32[]{:S(2)}) collective-permute-start(bf16[8,256,128]{2,1,0:T(8,128)(2,1)S(1)} %slice.24), channel_id=1, source_target_pairs={{2,0},{4,2},{6,4},{8,6},{10,8},{12,10},{14,12},{16,14},{18,16},{20... | collective-permute-start | bytes 1572872 | tf_op jit(solution)/shard_map/ppermute | solution.py:10
  (4 other events, 10.9 us)
Sparse Core Ops, SparseCore 0:
  150.1 20.8 reduce-scatter.2
  173.4 20.3 reduce-scatter.4
where the time goes:
time: 205 us; the launch traced here: 203 us
  matrix products  98.8 us (48%)
  waiting for transfers between devices  47.2 us (23%)
  local copies, waits for them, and re-layouts  16.2 us (8%)
  other arithmetic  14.3 us (7%)
  between operations  14.3 us (7%)
  starting transfers between devices  11.6 us (6%)
    dot_general x8, matrix products, full_group(): jnp.einsum('rqk,qrd->kd', attn_low, dout_grp, preferred_element_type=jnp....  23.9 us
    reduce_scatter x1, waiting for transfers between devices, per_device(): lax.psum_scatter(value_total, 'tp', scatter_dimension=0, tiled=True)  20.7 us
    dot_general x8, matrix products, group_grads(): jnp.einsum('rqk,kd->qrd', attn_low, value_window, preferred_element_type=...  19.7 us
    dot_general x8, matrix products, group_grads(): jnp.einsum('qrd,kd->rqk', dout_grp, value_window, preferred_element_type=...  17.9 us
    sub x8, matrix products, group_grads(): shifted = jnp.exp(scores - row_max)  17.8 us
    ppermute x4, waiting for transfers between devices, passed_along(): return lax.ppermute(block, axis, route)  17.6 us
    dot_general x8, matrix products, full_group(): jnp.einsum('rqk,qrd->kd', grad_low, query_grp, preferred_element_type=jnp...  16.8 us
    ppermute x4, starting transfers between devices, passed_along(): return lax.ppermute(block, axis, route)  11.5 us
  transfers between devices with their start and end apart: 6, of which 5 were waited for; matrix products, arithmetic and copies ran while one was open for 6% of the time, Pallas kernels for 0%

commit v1 on v0

v1 whole, which is shorter than its diff:
```python
import functools
import math
import jax
import jax.numpy as jnp
from jax import lax
from jax.experimental import pallas as pl
from jax.experimental.pallas import tpu as pltpu
from jax.sharding import PartitionSpec as P

F32 = jnp.float32
BF16 = jnp.bfloat16
NT = (((1,), (1,)), ((), ()))
TN = (((0,), (0,)), ((), ()))


def passed_along(block, axis, distance):
    devices = range(lax.axis_size(axis))
    route = [(i - distance, i) for i in devices if i - distance in devices]
    return lax.ppermute(block, axis, route)


def fill_bias(bias, lengths, first, heads, chunk):
    chunks, keys, rows = bias.shape
    for j in range(chunks):
        query_pos = first + chunk * j + lax.broadcasted_iota(jnp.int32, (1, rows), 1) // heads

        def step(d, carry):
            end, start = carry
            end = end + lengths[d]
            return end, jnp.where(query_pos >= end, end, start)

        _, start = lax.fori_loop(
            0, lengths.shape[0], step, (jnp.int32(0), jnp.zeros((1, rows), jnp.int32))
        )
        key_pos = first + chunk * (j + 1) - keys + lax.broadcasted_iota(jnp.int32, (keys, rows), 0)
        allowed = (key_pos >= start) & (key_pos <= query_pos)
        bias[j] = jnp.where(allowed, 0.0, -1e30).astype(F32)


def row_factor(exponents, block, group, heads, rows):
    head = lax.broadcasted_iota(jnp.int32, (1, rows), 1) % heads
    level = jnp.full((1, rows), exponents[block, group, 0], jnp.int32)
    for r in range(1, heads):
        level = jnp.where(head == r, exponents[block, group, r], level)
    factor = jnp.full((1, rows), 1.0, F32)
    for value in (-2, -1, 1, 2):
        factor = jnp.where(level == value, 2.0**value, factor)
    return factor


def group_terms(query, grad, key_ref, value_ref, bias, factors, grad_key, grad_value):
    chunks, keys, rows = bias.shape
    chunk = (key_ref.shape[0] - keys) // (chunks - 1)
    scaling = query.shape[1] ** -0.5
    grad_key[...] = jnp.zeros_like(grad_key)
    grad_value[...] = jnp.zeros_like(grad_value)
    grad_query = []
    for j in range(chunks):
        window = pl.ds(chunk * j, keys)
        q = query[rows * j : rows * (j + 1)]
        g = grad[rows * j : rows * (j + 1)]
        k = key_ref[window]
        v = value_ref[window]
        scores = lax.dot_general(k, q, NT, preferred_element_type=F32) + bias[j]
        top = jnp.max(scores, axis=0, keepdims=True)
        e = jnp.exp2((scores - top) * (scaling * math.log2(math.e)))
        inverse = 1.0 / jnp.sum(e, axis=0, keepdims=True)
        grad_probs = lax.dot_general(v, g, NT, preferred_element_type=F32)
        delta = jnp.sum(e * grad_probs, axis=0, keepdims=True) * inverse
        p = e * (inverse * factors[j] * scaling)
        low = p.astype(BF16)
        ds = (p * (grad_probs - delta)).astype(BF16)
        grad_query.append(lax.dot_general(ds, k, TN, preferred_element_type=F32).astype(BF16))
        grad_key[window] += jnp.dot(ds, q, preferred_element_type=F32)
        grad_value[window] += jnp.dot(low, g, preferred_element_type=F32)
    return jnp.concatenate(grad_query, axis=0)


def local_kernel(
    chunk, lengths, exponents, q_ref, go_ref, pk_ref, pv_ref, k_ref, v_ref,
    gq_ref, own_k, own_v, back_k, back_v, wide, key_win, value_win, bias, acc_k, acc_v,
):
    group = pl.program_id(0)
    tokens, groups, width = k_ref.shape
    heads = q_ref.shape[2]
    first = lax.axis_index("seq") * tokens

    @pl.when(group == 0)
    def _():
        fill_bias(bias, lengths, first, heads, chunk)
        for src, dst, at in (
            (pk_ref, key_win, 0), (k_ref, key_win, tokens),
            (pv_ref, value_win, 0), (v_ref, value_win, tokens),
        ):
            wide[...] = src[...].astype(F32).reshape(tokens * groups, width)
            for i in range(groups):
                dst[i, pl.ds(at, tokens)] = wide[pl.ds(i, tokens, stride=groups)].astype(BF16)

    chunks, _, rows = bias.shape
    blocks = exponents.shape[0]
    factors = [
        row_factor(exponents, (j * blocks) // chunks, group, heads, rows) for j in range(chunks)
    ]
    out = group_terms(
        q_ref[...].reshape(tokens * heads, width), go_ref[...].reshape(tokens * heads, width),
        key_win.at[group], value_win.at[group], bias, factors, acc_k, acc_v,
    )
    gq_ref[...] = out.reshape(tokens, 1, heads, width)
    back_k[...] = acc_k[:tokens].astype(BF16)
    own_k[...] = acc_k[tokens:]
    back_v[...] = (acc_v[:tokens] * width**0.5).astype(BF16)
    own_v[...] = acc_v[tokens:] * width**0.5


def per_device(queries, keys, values, grad_out, exponents, lengths):
    tokens, groups, heads, width = queries.shape
    chunks = 4
    chunk = tokens // chunks
    window = tokens + chunk
    pk, pv = passed_along((keys, values), "seq", 1)
    smem = pl.BlockSpec(memory_space=pltpu.SMEM)
    vmem = pl.BlockSpec(memory_space=pltpu.VMEM)
    rows_spec = pl.BlockSpec((tokens, 1, heads, width), lambda g: (0, g, 0, 0))
    term_spec = pl.BlockSpec((None, tokens, width), lambda g: (g, 0, 0))
    gq, own_k, own_v, back_k, back_v = pl.pallas_call(
        functools.partial(local_kernel, chunk),
        grid=(groups,),
        in_specs=[smem, smem, rows_spec, rows_spec, vmem, vmem, vmem, vmem],
        out_specs=[rows_spec, term_spec, term_spec, term_spec, term_spec],
        out_shape=[
            jax.ShapeDtypeStruct(queries.shape, BF16),
            jax.ShapeDtypeStruct((groups, tokens, width), F32),
            jax.ShapeDtypeStruct((groups, tokens, width), F32),
            jax.ShapeDtypeStruct((groups, tokens, width), BF16),
            jax.ShapeDtypeStruct((groups, tokens, width), BF16),
        ],
        scratch_shapes=[
            pltpu.VMEM((tokens * groups, width), F32),
            pltpu.VMEM((groups, 2 * tokens, width), BF16),
            pltpu.VMEM((groups, 2 * tokens, width), BF16),
            pltpu.VMEM((chunks, window, chunk * heads), F32),
            pltpu.VMEM((2 * tokens, width), F32),
            pltpu.VMEM((2 * tokens, width), F32),
        ],
        compiler_params=pltpu.CompilerParams(vmem_limit_bytes=48 * 1024 * 1024),
    )(lengths, exponents, queries, grad_out, pk, pv, keys, values)
    key_total = own_k + passed_along(back_k, "seq", -1).astype(F32)
    value_total = own_v + passed_along(back_v, "seq", -1).astype(F32)
    summed_keys, summed_values = (
        lax.psum_scatter(key_total, "tp", scatter_dimension=0, tiled=True),
        lax.psum_scatter(value_total, "tp", scatter_dimension=0, tiled=True),
    )
    return (
        gq,
        jnp.moveaxis(summed_keys, 0, 1).astype(BF16),
        jnp.moveaxis(summed_values, 0, 1).astype(BF16),
    )


def solution(mesh):
    placed = (
        P("seq", None, "tp", None),
        P("seq", None, None),
        P("seq", None, None),
        P("seq", None, "tp", None),
        P("seq", None, "tp"),
        P(),
    )
    return jax.shard_map(
        per_device,
        mesh=mesh,
        in_specs=placed,
        out_specs=(P("seq", None, "tp", None), P("seq", "tp", None), P("seq", "tp", None)),
        check_vma=False,
    )
```

time: 205 us -> 114 us (0.56)
  matrix products: 98.8 us -> 0 us
  Pallas kernels: 0 us -> 21.6 us
  local copies, waits for them, and re-layouts: 16.2 us -> 5.32 us
  waiting for transfers between devices: 47.2 us -> 57.2 us
  other arithmetic: 14.3 us -> 4.33 us
    dot_general x40 -> x0, matrix products: 81 us -> none  [the longest x8 23.9 us: full_group(): jnp.einsum('rqk,qrd->kd', attn_low, dout_grp, preferred_element_type=jnp....]
    pallas_call x0 -> x1, Pallas kernels: none -> 21.6 us  [per_device(): pl.pallas_call(functools.partial(local_kernel, chunk), grid=(groups,), in...]
    sub x8 -> x0, matrix products: 17.8 us -> none  [group_grads(): shifted = jnp.exp(scores - row_max)]
    ppermute x4, waiting for transfers between devices: 17.6 us -> 27.5 us  [passed_along(): return lax.ppermute(block, axis, route)]
    dynamic_update_slice x16 -> x0, local copies, waits for them, and re-layouts: 7.77 us -> none  [core_grads(): lax.map(full_group, (query_major, dout_major, key_window, value_window))]
    transpose x3 -> x0, other arithmetic: 6.15 us -> none  [the longest x1 2.88 us: core_grads(): dout_major = jnp.moveaxis(scaled, 1, 0)]
    and x8 -> x0, other arithmetic: 2.15 us -> none  [core_grads(): (query_doc[:, None] == key_doc[None, :]) & (key_pos[None, :] <= query_pos...]
    unnamed x17 -> x9, local copies, waits for them, and re-layouts: 6.62 us -> 5.32 us
  transfers between devices with their start and end apart: 6 -> 6, of which waited for: 5 -> 6; matrix products, arithmetic and copies ran while one was open for 6% -> 3% of each run, Pallas kernels for 0% -> 0%
where the time goes in v1:
time: 114 us; the launch traced here: 113 us
  waiting for transfers between devices  57.2 us (50%)
  Pallas kernels  21.6 us (19%)
  between operations  14.1 us (12%)
  starting transfers between devices  10.4 us (9%)
  local copies, waits for them, and re-layouts  5.32 us (5%)
  other arithmetic  4.33 us (4%)
    ppermute x4, waiting for transfers between devices, passed_along(): return lax.ppermute(block, axis, route)  27.5 us
    pallas_call x1, Pallas kernels, per_device(): pl.pallas_call(functools.partial(local_kernel, chunk), grid=(groups,), in...  21.6 us
    reduce_scatter x1, waiting for transfers between devices, per_device(): lax.psum_scatter(value_total, 'tp', scatter_dimension=0, tiled=True)  20.7 us
    ppermute x4, starting transfers between devices, passed_along(): return lax.ppermute(block, axis, route)  10.3 us
    reduce_scatter x1, waiting for transfers between devices, per_device(): lax.psum_scatter(key_total, 'tp', scatter_dimension=0, tiled=True)  8.97 us
    unnamed x9, local copies, waits for them, and re-layouts  5.32 us
  transfers between devices with their start and end apart: 6, of which 6 were waited for; matrix products, arithmetic and copies ran while one was open for 3% of the time, Pallas kernels for 0%

profile of v1, /device:TPU:1, one launch (start us, length us, event | category | flops | bytes accessed | tf_op | source)
XLA Modules:
  0.0 112.9 jit_solution(15626210140906457709)
XLA Ops:
  7.2 0.0 reduce-scatter.3.cloned.1.call-start
  7.2 4.5 %collective-permute-start = (bf16[256,8,128]{2,1,0:T(8,128)(2,1)}, bf16[256,8,128]{2,1,0:T(8,128)(2,1)S(1)}, u32[]{:S(2)}, u32[]{:S(2)}) collective-permute-start(bf16[256,8,128]{2,1,0:T(8,128)(2,1)} %k_ref.1), channel_id=1, source_target_pairs={{0,2},{2,4},{4,6},{6,8},{8,10},{10,12},{12,14},{14,16},{16,18},{18... | collective-permute-start | bytes 1572872 | tf_op jit(solution)/shard_map/ppermute | solution.py:19
  11.8 1.9 %collective-permute-start.1 = (bf16[256,8,128]{2,1,0:T(8,128)(2,1)}, bf16[256,8,128]{2,1,0:T(8,128)(2,1)S(1)}, u32[]{:S(2)}, u32[]{:S(2)}) collective-permute-start(bf16[256,8,128]{2,1,0:T(8,128)(2,1)} %v_ref.1), channel_id=1, source_target_pairs={{0,2},{2,4},{4,6},{6,8},{8,10},{10,12},{12,14},{14,16},{16,18},{18... | collective-permute-start | bytes 1572872 | tf_op jit(solution)/shard_map/ppermute | solution.py:19
  13.7 0.8 copy.9.exponents
  14.5 3.7 %collective-permute-done.pk_ref = bf16[256,8,128]{2,1,0:T(8,128)(2,1)S(1)} collective-permute-done((bf16[256,8,128]{2,1,0:T(8,128)(2,1)}, bf16[256,8,128]{2,1,0:T(8,128)(2,1)S(1)}, u32[]{:S(2)}, u32[]{:S(2)}) %collective-permute-start) | collective-permute-done | bytes 524320 | tf_op jit(solution)/shard_map/ppermute | solution.py:19
  18.2 5.6 %collective-permute-done.1.pv_ref = bf16[256,8,128]{2,1,0:T(8,128)(2,1)S(1)} collective-permute-done((bf16[256,8,128]{2,1,0:T(8,128)(2,1)}, bf16[256,8,128]{2,1,0:T(8,128)(2,1)S(1)}, u32[]{:S(2)}, u32[]{:S(2)}) %collective-permute-start.1) | collective-permute-done | bytes 524320 | tf_op jit(solution)/shard_map/ppermute | solution.py:19
  23.8 1.0 copy-done
  24.8 1.0 copy-done.1
  25.9 0.7 copy-done.2
  26.5 21.6 %shard_map.85 = (bf16[256,8,4,128]{3,2,1,0:T(4,128)(2,1)}, f32[8,256,128]{2,1,0:T(8,128)S(1)}, f32[8,256,128]{2,1,0:T(8,128)S(1)}, bf16[8,256,128]{2,1,0:T(8,128)(2,1)S(1)}, bf16[8,256,128]{2,1,0:T(8,128)(2,1)S(1)}) custom-call(s32[32]{0:T(128)S(1)} %copy-done.2, s32[2,8,4]{2,1,0:T(8,128)S(1)} %copy.9.exponents, bf16[256,8,4,128]{3,2,1,0:T(4,128)(2,1)} %q_ref.1, ...), custom_call_target="tpu_custom_call" | custom-call | tf_op jit(solution)/shard_map/pallas_call | solution.py:125
  48.1 1.9 %collective-permute-start.2 = (bf16[8,256,128]{2,1,0:T(8,128)(2,1)S(1)}, bf16[8,256,128]{2,1,0:T(8,128)(2,1)S(1)}, u32[]{:S(2)}, u32[]{:S(2)}) collective-permute-start(bf16[8,256,128]{2,1,0:T(8,128)(2,1)S(1)} %get-tuple-element.10), channel_id=1, source_target_pairs={{2,0},{4,2},{6,4},{8,6},{10,8},{12,10},{14,12},{16,14},{18,16},{20... | collective-permute-start | bytes 1572872 | tf_op jit(solution)/shard_map/ppermute | solution.py:19
  50.0 9.2 %collective-permute-done.2 = bf16[8,256,128]{2,1,0:T(8,128)(2,1)S(1)} collective-permute-done((bf16[8,256,128]{2,1,0:T(8,128)(2,1)S(1)}, bf16[8,256,128]{2,1,0:T(8,128)(2,1)S(1)}, u32[]{:S(2)}, u32[]{:S(2)}) %collective-permute-start.2) | collective-permute-done | bytes 524320 | tf_op jit(solution)/shard_map/ppermute | solution.py:19
  59.2 1.1 convert_add_fusion.1
  60.3 0.0 reduce-scatter.5.cloned.1.call-start
  60.4 1.9 %collective-permute-start.3 = (bf16[8,256,128]{2,1,0:T(8,128)(2,1)S(1)}, bf16[8,256,128]{2,1,0:T(8,128)(2,1)S(1)}, u32[]{:S(2)}, u32[]{:S(2)}) collective-permute-start(bf16[8,256,128]{2,1,0:T(8,128)(2,1)S(1)} %get-tuple-element.12), channel_id=1, source_target_pairs={{2,0},{4,2},{6,4},{8,6},{10,8},{12,10},{14,12},{16,14},{18,16},{20... | collective-permute-start | bytes 1572872 | tf_op jit(solution)/shard_map/ppermute | solution.py:19
  62.3 9.0 %collective-permute-done.3 = bf16[8,256,128]{2,1,0:T(8,128)(2,1)S(1)} collective-permute-done((bf16[8,256,128]{2,1,0:T(8,128)(2,1)S(1)}, bf16[8,256,128]{2,1,0:T(8,128)(2,1)S(1)}, u32[]{:S(2)}, u32[]{:S(2)}) %collective-permute-start.3) | collective-permute-done | bytes 524320 | tf_op jit(solution)/shard_map/ppermute | solution.py:19
  71.3 1.1 convert_add_fusion
  72.4 0.0 reduce-scatter.5.cloned.1.call-update
  72.4 9.0 %reduce-scatter.3.cloned.1.call-done = f32[4,256,128]{2,1,0:T(8,128)} async-done(((f32[8,256,128]{2,1,0:T(8,128)}), f32[4,256,128]{2,1,0:T(8,128)}) %reduce-scatter.3.cloned.1.call-update) | async-done | bytes 524304 | tf_op jit(solution)/shard_map/reduce_scatter | solution.py:150
  81.4 1.1 convert_bitcast_fusion.1
  82.4 0.9 copy.10
  83.4 20.7 %reduce-scatter.5.cloned.1.call-done = f32[4,256,128]{2,1,0:T(8,128)} async-done(((f32[8,256,128]{2,1,0:T(8,128)}), f32[4,256,128]{2,1,0:T(8,128)}) %reduce-scatter.5.cloned.1.call-update) | async-done | bytes 524304 | tf_op jit(solution)/shard_map/reduce_scatter | solution.py:151
  104.0 1.1 convert_bitcast_fusion
  105.1 0.9 copy.11
  (4 shorter events, 0.0 us)
Async XLA Ops:
  7.2 74.2 %reduce-scatter.3.cloned.1.call-start = ((), (), s32[]{:S(2)}) async-start(), calls=%async_computation.2 | async-start | bytes 1572864 | tf_op jit(solution)/shard_map/reduce_scatter | solution.py:150
  7.2 11.0 %collective-permute-start = (bf16[256,8,128]{2,1,0:T(8,128)(2,1)}, bf16[256,8,128]{2,1,0:T(8,128)(2,1)S(1)}, u32[]{:S(2)}, u32[]{:S(2)}) collective-permute-start(bf16[256,8,128]{2,1,0:T(8,128)(2,1)} %k_ref.1), channel_id=1, source_target_pairs={{0,2},{2,4},{4,6},{6,8},{8,10},{10,12},{12,14},{14,16},{16,18},{18... | collective-permute-start | bytes 1572872 | tf_op jit(solution)/shard_map/ppermute | solution.py:19
  11.8 12.0 %collective-permute-start.1 = (bf16[256,8,128]{2,1,0:T(8,128)(2,1)}, bf16[256,8,128]{2,1,0:T(8,128)(2,1)S(1)}, u32[]{:S(2)}, u32[]{:S(2)}) collective-permute-start(bf16[256,8,128]{2,1,0:T(8,128)(2,1)} %v_ref.1), channel_id=1, source_target_pairs={{0,2},{2,4},{4,6},{6,8},{8,10},{10,12},{12,14},{14,16},{16,18},{18... | collective-permute-start | bytes 1572872 | tf_op jit(solution)/shard_map/ppermute | solution.py:19
  23.8 1.0 copy-start
  24.8 1.0 copy-start.1
  25.9 0.7 copy-start.2
  48.1 11.1 %collective-permute-start.2 = (bf16[8,256,128]{2,1,0:T(8,128)(2,1)S(1)}, bf16[8,256,128]{2,1,0:T(8,128)(2,1)S(1)}, u32[]{:S(2)}, u32[]{:S(2)}) collective-permute-start(bf16[8,256,128]{2,1,0:T(8,128)(2,1)S(1)} %get-tuple-element.10), channel_id=1, source_target_pairs={{2,0},{4,2},{6,4},{8,6},{10,8},{12,10},{14,12},{16,14},{18,16},{20... | collective-permute-start | bytes 1572872 | tf_op jit(solution)/shard_map/ppermute | solution.py:19
  60.3 43.7 %reduce-scatter.5.cloned.1.call-start = ((), (), s32[]{:S(2)}) async-start(), calls=%async_computation.3 | async-start | bytes 1572864 | tf_op jit(solution)/shard_map/reduce_scatter | solution.py:151
  60.4 10.9 %collective-permute-start.3 = (bf16[8,256,128]{2,1,0:T(8,128)(2,1)S(1)}, bf16[8,256,128]{2,1,0:T(8,128)(2,1)S(1)}, u32[]{:S(2)}, u32[]{:S(2)}) collective-permute-start(bf16[8,256,128]{2,1,0:T(8,128)(2,1)S(1)} %get-tuple-element.12), channel_id=1, source_target_pairs={{2,0},{4,2},{6,4},{8,6},{10,8},{12,10},{14,12},{16,14},{18,16},{20... | collective-permute-start | bytes 1572872 | tf_op jit(solution)/shard_map/ppermute | solution.py:19
Sparse Core Ops, SparseCore 0:
  60.4 20.8 reduce-scatter.2
  83.7 20.3 reduce-scatter.4

commit v2 on v1

v2 whole, which is shorter than its diff:
```python
import functools
import math
import jax
import jax.numpy as jnp
from jax import lax
from jax.experimental import pallas as pl
from jax.experimental.pallas import tpu as pltpu
from jax.sharding import PartitionSpec as P

F32 = jnp.float32
BF16 = jnp.bfloat16
NT = (((1,), (1,)), ((), ()))
TN = (((0,), (0,)), ((), ()))
MESH = pl.DeviceIdType.MESH
LAG = 1


def fill_bias(bias, lengths, first, heads, chunk):
    chunks, keys, rows = bias.shape
    for j in range(chunks):
        query_pos = first + chunk * j + lax.broadcasted_iota(jnp.int32, (1, rows), 1) // heads

        def step(d, carry):
            end, start = carry
            end = end + lengths[d]
            return end, jnp.where(query_pos >= end, end, start)

        _, start = lax.fori_loop(
            0, lengths.shape[0], step, (jnp.int32(0), jnp.zeros((1, rows), jnp.int32))
        )
        key_pos = first + chunk * (j + 1) - keys + lax.broadcasted_iota(jnp.int32, (keys, rows), 0)
        allowed = (key_pos >= start) & (key_pos <= query_pos)
        bias[j] = jnp.where(allowed, 0.0, -1e30).astype(F32)


def row_factor(exponents, block, group, heads, rows):
    head = lax.broadcasted_iota(jnp.int32, (1, rows), 1) % heads
    level = jnp.full((1, rows), exponents[block, 0, group], jnp.int32)
    for r in range(1, heads):
        level = jnp.where(head == r, exponents[block, r, group], level)
    factor = jnp.full((1, rows), 1.0, F32)
    for value in (-2, -1, 1, 2):
        factor = jnp.where(level == value, 2.0**value, factor)
    return factor


def group_terms(query, grad, key_ref, value_ref, bias, factors, grad_key, grad_value):
    chunks, keys, rows = bias.shape
    chunk = (key_ref.shape[0] - keys) // (chunks - 1)
    scaling = query.shape[1] ** -0.5
    grad_key[...] = jnp.zeros_like(grad_key)
    grad_value[...] = jnp.zeros_like(grad_value)
    grad_query = []
    for j in range(chunks):
        window = pl.ds(chunk * j, keys)
        q = query[rows * j : rows * (j + 1)]
        g = grad[rows * j : rows * (j + 1)]
        k = key_ref[window]
        v = value_ref[window]
        scores = lax.dot_general(k, q, NT, preferred_element_type=F32) + bias[j]
        top = jnp.max(scores, axis=0, keepdims=True)
        e = jnp.exp2((scores - top) * (scaling * math.log2(math.e)))
        inverse = 1.0 / jnp.sum(e, axis=0, keepdims=True)
        grad_probs = lax.dot_general(v, g, NT, preferred_element_type=F32)
        delta = jnp.sum(e * grad_probs, axis=0, keepdims=True) * inverse
        p = e * (inverse * factors[j] * scaling)
        low = p.astype(BF16)
        ds = (p * (grad_probs - delta)).astype(BF16)
        grad_query.append(lax.dot_general(ds, k, TN, preferred_element_type=F32).astype(BF16))
        grad_key[window] += jnp.dot(ds, q, preferred_element_type=F32)
        grad_value[window] += jnp.dot(low, g, preferred_element_type=F32)
    return jnp.concatenate(grad_query, axis=0)


def group_at(i, rank, ranks, share):
    return lax.rem(rank + 1 + i // share, ranks) * share + lax.rem(i, share)


def fused_kernel(
    chunk, shards, ranks,
    lengths, exponents, q_ref, go_ref, k_ref, v_ref,
    gq_ref, gk_ref, gv_ref,
    wide_k, wide_v, own_k, own_v, prev_k, prev_v, window_k, window_v, bias,
    acc_k, acc_v, own, back_out, back_in, cross_out, cross_in, out_k, out_v,
    win_send, win_recv, back_send, back_recv, cross_send, cross_recv,
):
    tokens, groups, width = k_ref.shape
    heads = q_ref.shape[2]
    share = groups // ranks
    foreign = groups - share
    shard, rank = lax.axis_index("seq"), lax.axis_index("tp")
    has_next, has_prev = shard < shards - 1, shard > 0
    unscale = width**0.5
    i = pl.program_id(0)
    group = group_at(i, rank, ranks, share)

    def window_copies(i):
        return [
            pltpu.make_async_remote_copy(
                src_ref=src.at[i], dst_ref=dst.at[i],
                send_sem=win_send.at[part, i], recv_sem=win_recv.at[part, i],
                device_id=(shard + 1, rank), device_id_type=MESH,
            )
            for part, (src, dst) in enumerate(((own_k, prev_k), (own_v, prev_v)))
        ]

    def back_copy(i):
        return pltpu.make_async_remote_copy(
            src_ref=back_out.at[i], dst_ref=back_in.at[i],
            send_sem=back_send.at[i], recv_sem=back_recv.at[i],
            device_id=(shard - 1, rank), device_id_type=MESH,
        )

    def cross_copy(i):
        return pltpu.make_async_remote_copy(
            src_ref=cross_out.at[i], dst_ref=cross_in.at[i],
            send_sem=cross_send.at[i], recv_sem=cross_recv.at[i],
            device_id=(shard, lax.rem(rank + 1 + i // share, ranks)), device_id_type=MESH,
        )

    @pl.when(i == 0)
    def _():
        barrier = pltpu.get_barrier_semaphore()

        @pl.when(has_next)
        def _():
            pl.semaphore_signal(barrier, inc=1, device_id=(shard + 1, rank), device_id_type=MESH)

        @pl.when(has_prev)
        def _():
            pl.semaphore_signal(barrier, inc=1, device_id=(shard - 1, rank), device_id_type=MESH)

        for other in range(1, ranks):
            peer = lax.rem(rank + other, ranks)
            pl.semaphore_signal(barrier, inc=1, device_id=(shard, peer), device_id_type=MESH)
        wide_k[...] = k_ref[...].astype(F32).reshape(tokens * groups, width)
        wide_v[...] = v_ref[...].astype(F32).reshape(tokens * groups, width)
        for n in range(groups):
            rows = pl.ds(group_at(n, rank, ranks, share), tokens, stride=groups)
            own_k[n] = wide_k[rows].astype(BF16)
            own_v[n] = wide_v[rows].astype(BF16)
        pl.semaphore_wait(
            barrier, ranks - 1 + has_next.astype(jnp.int32) + has_prev.astype(jnp.int32)
        )

        @pl.when(has_next)
        def _():
            for n in range(groups):
                for copy in window_copies(n):
                    copy.start()

        fill_bias(bias, lengths, shard * tokens, heads, chunk)

    chunks, _, rows = bias.shape
    blocks = exponents.shape[0]

    def add_back(i):
        @pl.when(has_next)
        def _():
            back_copy(i).wait_recv()
            own[i] += back_in[i].astype(F32)

    def pass_on(i):
        add_back(i)
        cross_out[i] = own[i].astype(BF16)
        cross_copy(i).start()

    def finish(i):
        add_back(i)
        local = i - foreign
        total = own[i]
        for other in range(ranks - 1):
            cross_copy(other * share + local).wait_recv()
            total = total + cross_in[other * share + local].astype(F32)
        out_k[pl.ds(local, tokens, stride=share)] = total[0]
        out_v[pl.ds(local, tokens, stride=share)] = total[1]

    @pl.when(has_prev)
    def _():
        for copy in window_copies(i):
            copy.wait_recv()
        window_k[:tokens] = prev_k[i]
        window_v[:tokens] = prev_v[i]

    @pl.when(jnp.logical_not(has_prev))
    def _():
        window_k[:tokens] = jnp.zeros((tokens, width), BF16)
        window_v[:tokens] = jnp.zeros((tokens, width), BF16)

    window_k[tokens:] = own_k[i]
    window_v[tokens:] = own_v[i]
    factors = [
        row_factor(exponents, (j * blocks) // chunks, group, heads, rows) for j in range(chunks)
    ]
    out = group_terms(
        q_ref[...].reshape(tokens * heads, width), go_ref[...].reshape(tokens * heads, width),
        window_k, window_v, bias, factors, acc_k, acc_v,
    )
    gq_ref[...] = out.reshape(tokens, 1, heads, width)
    own[i, 0] = acc_k[tokens:]
    own[i, 1] = acc_v[tokens:] * unscale

    @pl.when(has_prev)
    def _():
        back_out[i, 0] = acc_k[:tokens].astype(BF16)
        back_out[i, 1] = (acc_v[:tokens] * unscale).astype(BF16)
        back_copy(i).start()

    @pl.when(jnp.logical_and(i >= LAG, i < foreign + LAG))
    def _():
        pass_on(i - LAG)

    @pl.when(i >= foreign + LAG)
    def _():
        finish(i - LAG)

    @pl.when(i == groups - 1)
    def _():
        for n in range(groups - LAG, groups):
            finish(n)
        gk_ref[...] = out_k[...].astype(BF16).reshape(tokens, share, width)
        gv_ref[...] = out_v[...].astype(BF16).reshape(tokens, share, width)

        @pl.when(has_next)
        def _():
            for n in range(groups):
                for copy in window_copies(n):
                    copy.wait_send()

        @pl.when(has_prev)
        def _():
            for n in range(groups):
                back_copy(n).wait_send()

        for n in range(foreign):
            cross_copy(n).wait_send()


def per_device(shards, ranks, queries, keys, values, grad_out, exponents, lengths):
    tokens, groups, heads, width = queries.shape
    chunks = 4
    chunk = tokens // chunks
    share = groups // ranks
    foreign = groups - share
    levels = jnp.swapaxes(exponents, 1, 2)
    smem = pl.BlockSpec(memory_space=pltpu.SMEM)
    vmem = pl.BlockSpec(memory_space=pltpu.VMEM)
    rows_spec = pl.BlockSpec(
        (tokens, 1, heads, width),
        lambda i: (0, group_at(i, lax.axis_index("tp"), ranks, share), 0, 0),
    )
    pair = (2, tokens, width)
    dma = pltpu.SemaphoreType.DMA
    return pl.pallas_call(
        functools.partial(fused_kernel, chunk, shards, ranks),
        grid=(groups,),
        in_specs=[smem, smem, rows_spec, rows_spec, vmem, vmem],
        out_specs=[rows_spec, vmem, vmem],
        out_shape=[
            jax.ShapeDtypeStruct(queries.shape, BF16),
            jax.ShapeDtypeStruct((tokens, share, width), BF16),
            jax.ShapeDtypeStruct((tokens, share, width), BF16),
        ],
        scratch_shapes=[
            pltpu.VMEM((tokens * groups, width), F32),
            pltpu.VMEM((tokens * groups, width), F32),
            pltpu.VMEM((groups, tokens, width), BF16),
            pltpu.VMEM((groups, tokens, width), BF16),
            pltpu.VMEM((groups, tokens, width), BF16),
            pltpu.VMEM((groups, tokens, width), BF16),
            pltpu.VMEM((2 * tokens, width), BF16),
            pltpu.VMEM((2 * tokens, width), BF16),
            pltpu.VMEM((chunks, tokens + chunk, chunk * heads), F32),
            pltpu.VMEM((2 * tokens, width), F32),
            pltpu.VMEM((2 * tokens, width), F32),
            pltpu.VMEM((groups,) + pair, F32),
            pltpu.VMEM((groups,) + pair, BF16),
            pltpu.VMEM((groups,) + pair, BF16),
            pltpu.VMEM((foreign,) + pair, BF16),
            pltpu.VMEM((foreign,) + pair, BF16),
            pltpu.VMEM((tokens * share, width), F32),
            pltpu.VMEM((tokens * share, width), F32),
            dma((2, groups)), dma((2, groups)), dma((groups,)), dma((groups,)),
            dma((foreign,)), dma((foreign,)),
        ],
        compiler_params=pltpu.CompilerParams(
            collective_id=0, has_side_effects=True, vmem_limit_bytes=60 * 1024 * 1024
        ),
    )(lengths, levels, queries, grad_out, keys, values)


def solution(mesh):
    placed = (
        P("seq", None, "tp", None),
        P("seq", None, None),
        P("seq", None, None),
        P("seq", None, "tp", None),
        P("seq", None, "tp"),
        P(),
    )
    return jax.shard_map(
        functools.partial(per_device, mesh.shape["seq"], mesh.shape["tp"]),
        mesh=mesh,
        in_specs=placed,
        out_specs=(P("seq", None, "tp", None), P("seq", "tp", None), P("seq", "tp", None)),
        check_vma=False,
    )
```

time: 114 us -> 43.2 us (0.38)
  the two profiles are of different devices: /device:TPU:1 before, /device:TPU:21 now
where the time goes in v2:
time: 43.2 us; the launch traced here: 43.1 us
  Pallas kernels  37.3 us (86%)
  local copies, waits for them, and re-layouts  5.1 us (12%)
  between operations  0.66 us (2%)
    pallas_call x1, Pallas kernels, per_device(): pl.pallas_call(functools.partial(fused_kernel, chunk, shards, ranks), gri...  37.3 us
    unnamed x7, local copies, waits for them, and re-layouts  5.1 us

profile of v2, /device:TPU:21, one launch (start us, length us, event | category | flops | bytes accessed | tf_op | source)
XLA Modules:
  0.0 43.1 jit_solution(17995519320719201383)
XLA Ops:
  0.6 37.3 %shard_map.85 = (bf16[256,8,4,128]{3,2,1,0:T(4,128)(2,1)}, bf16[256,4,128]{2,1,0:T(4,128)(2,1)}, bf16[256,4,128]{2,1,0:T(4,128)(2,1)}) custom-call(s32[32]{0:T(128)} %lengths.1, s32[2,4,8]{2,1,0:T(4,128)} %bitcast.1, bf16[256,8,4,128]{3,2,1,0:T(4,128)(2,1)} %q_ref.1, bf16[256,8,4,128]{3,2,1,0:T(4,128)(2,1)} %go_ref.1, bf16[256,8,128]{2,1,0:T(8,128)(2,1)} %k_ref.1, ...), custom_call_target="tpu_custom_call" | custom-call | tf_op jit(solution)/shard_map/pallas_call | solution.py:254
  37.9 0.0 copy-start.1
  38.0 0.0 copy-start
  38.0 3.7 %copy.12 = bf16[256,8,4,128]{3,2,1,0:T(4,128)(2,1)} copy(bf16[256,8,4,128]{3,2,1,0:T(4,128)(2,1)} %get-tuple-element.6) | data formatting | bytes 4194304
  41.6 0.0 copy-done.1
  41.7 0.7 %copy.13 = bf16[256,4,128]{2,1,0:T(4,128)(2,1)} copy(bf16[256,4,128]{2,1,0:T(4,128)(2,1)S(1)} %copy-done.1) | data formatting | bytes 524288
  42.4 0.0 copy-done
  42.4 0.7 %copy.14 = bf16[256,4,128]{2,1,0:T(4,128)(2,1)} copy(bf16[256,4,128]{2,1,0:T(4,128)(2,1)S(1)} %copy-done) | data formatting | bytes 524288
Async XLA Ops:
  37.9 3.7 %copy-start.1 = (bf16[256,4,128]{2,1,0:T(4,128)(2,1)S(1)}, bf16[256,4,128]{2,1,0:T(4,128)(2,1)}, u32[]{:S(2)}) copy-start(bf16[256,4,128]{2,1,0:T(4,128)(2,1)} %get-tuple-element.7) | copy-start | bytes 786436
  38.0 4.4 %copy-start = (bf16[256,4,128]{2,1,0:T(4,128)(2,1)S(1)}, bf16[256,4,128]{2,1,0:T(4,128)(2,1)}, u32[]{:S(2)}) copy-start(bf16[256,4,128]{2,1,0:T(4,128)(2,1)} %get-tuple-element.8) | copy-start | bytes 786436

commit v3 on v2

--- a/solution.py
+++ b/solution.py
@@ -12,7 +12,8 @@
 NT = (((1,), (1,)), ((), ()))
 TN = (((0,), (0,)), ((), ()))
 MESH = pl.DeviceIdType.MESH
-LAG = 1
+AHEAD = 3
+LAG = 2
 
 
 def fill_bias(bias, lengths, first, heads, chunk):
@@ -104,6 +105,12 @@
             for part, (src, dst) in enumerate(((own_k, prev_k), (own_v, prev_v)))
         ]
 
+    def send_window(i):
+        @pl.when(has_next)
+        def _():
+            for copy in window_copies(i):
+                copy.start()
+
     def back_copy(i):
         return pltpu.make_async_remote_copy(
             src_ref=back_out.at[i], dst_ref=back_in.at[i],
@@ -139,17 +146,19 @@
             rows = pl.ds(group_at(n, rank, ranks, share), tokens, stride=groups)
             own_k[n] = wide_k[rows].astype(BF16)
             own_v[n] = wide_v[rows].astype(BF16)
-        pl.semaphore_wait(
-            barrier, ranks - 1 + has_next.astype(jnp.int32) + has_prev.astype(jnp.int32)
-        )
-
-        @pl.when(has_next)
-        def _():
-            for n in range(groups):
-                for copy in window_copies(n):
-                    copy.start()
-
+            if n == 0:
+                pl.semaphore_wait(
+                    barrier, ranks - 1 + has_next.astype(jnp.int32) + has_prev.astype(jnp.int32)
+                )
+                send_window(0)
+        send_window(1)
         fill_bias(bias, lengths, shard * tokens, heads, chunk)
+        for n in range(2, AHEAD):
+            send_window(n)
+
+    @pl.when(i + AHEAD < groups)
+    def _():
+        send_window(i + AHEAD)
 
     chunks, _, rows = bias.shape
     blocks = exponents.shape[0]
@@ -196,7 +205,7 @@
         q_ref[...].reshape(tokens * heads, width), go_ref[...].reshape(tokens * heads, width),
         window_k, window_v, bias, factors, acc_k, acc_v,
     )
-    gq_ref[...] = out.reshape(tokens, 1, heads, width)
+    gq_ref[:, pl.ds(group, 1)] = out.reshape(tokens, 1, heads, width)
     own[i, 0] = acc_k[tokens:]
     own[i, 1] = acc_v[tokens:] * unscale
 
@@ -255,11 +264,11 @@
         functools.partial(fused_kernel, chunk, shards, ranks),
         grid=(groups,),
         in_specs=[smem, smem, rows_spec, rows_spec, vmem, vmem],
-        out_specs=[rows_spec, vmem, vmem],
+        out_specs=[vmem] * 3,
         out_shape=[
-            jax.ShapeDtypeStruct(queries.shape, BF16),
-            jax.ShapeDtypeStruct((tokens, share, width), BF16),
-            jax.ShapeDtypeStruct((tokens, share, width), BF16),
+            pltpu.VMEM(queries.shape, BF16),
+            pltpu.VMEM((tokens, share, width), BF16),
+            pltpu.VMEM((tokens, share, width), BF16),
         ],
         scratch_shapes=[
             pltpu.VMEM((tokens * groups, width), F32),

time: 43.2 us -> 34.7 us (0.80)
  the two profiles are of different devices: /device:TPU:21 before, /device:TPU:1 now
where the time goes in v3:
time: 34.7 us; the launch traced here: 34.3 us
  Pallas kernels  31 us (89%)
  local copies, waits for them, and re-layouts  2.73 us (8%)
  between operations  0.64 us (2%)
    pallas_call x1, Pallas kernels, per_device(): pl.pallas_call(functools.partial(fused_kernel, chunk, shards, ranks), gri...  31 us
    unnamed x3, local copies, waits for them, and re-layouts  2.73 us

profile of v3, /device:TPU:1, one launch (start us, length us, event | category | flops | bytes accessed | tf_op | source)
XLA Modules:
  0.0 34.3 jit_solution(5319815955033488101)
XLA Ops:
  0.6 31.0 %shard_map.85 = (bf16[256,8,4,128]{3,2,1,0:T(4,128)(2,1)S(1)}, bf16[256,4,128]{2,1,0:T(4,128)(2,1)S(1)}, bf16[256,4,128]{2,1,0:T(4,128)(2,1)S(1)}) custom-call(s32[32]{0:T(128)} %lengths.1, s32[2,4,8]{2,1,0:T(4,128)} %bitcast.1, bf16[256,8,4,128]{3,2,1,0:T(4,128)(2,1)} %q_ref.1, bf16[256,8,4,128]{3,2,1,0:T(4,128)(2,1)} %go_ref.1, ...), custom_call_target="tpu_custom_call" | custom-call | tf_op jit(solution)/shard_map/pallas_call | solution.py:263
  31.6 1.3 %copy.12 = bf16[256,8,4,128]{3,2,1,0:T(4,128)(2,1)} copy(bf16[256,8,4,128]{3,2,1,0:T(4,128)(2,1)S(1)} %get-tuple-element.3) | data formatting | bytes 4194304
  32.9 0.7 %copy.13 = bf16[256,4,128]{2,1,0:T(4,128)(2,1)} copy(bf16[256,4,128]{2,1,0:T(4,128)(2,1)S(1)} %get-tuple-element.4) | data formatting | bytes 524288
  33.6 0.7 %copy.14 = bf16[256,4,128]{2,1,0:T(4,128)(2,1)} copy(bf16[256,4,128]{2,1,0:T(4,128)(2,1)S(1)} %get-tuple-element.5) | data formatting | bytes 524288

commit v4 on v3

--- a/solution.py
+++ b/solution.py
@@ -52,24 +52,39 @@
     grad_key[...] = jnp.zeros_like(grad_key)
     grad_value[...] = jnp.zeros_like(grad_value)
     grad_query = []
-    for j in range(chunks):
+
+    def operands(j):
         window = pl.ds(chunk * j, keys)
-        q = query[rows * j : rows * (j + 1)]
-        g = grad[rows * j : rows * (j + 1)]
-        k = key_ref[window]
-        v = value_ref[window]
+        mine = slice(rows * j, rows * (j + 1))
+        return window, query[mine], grad[mine], key_ref[window], value_ref[window]
+
+    def products(j):
+        _, q, g, k, v = operands(j)
         scores = lax.dot_general(k, q, NT, preferred_element_type=F32) + bias[j]
+        return scores, lax.dot_general(v, g, NT, preferred_element_type=F32)
+
+    def weights(j, scores, grad_probs):
         top = jnp.max(scores, axis=0, keepdims=True)
         e = jnp.exp2((scores - top) * (scaling * math.log2(math.e)))
         inverse = 1.0 / jnp.sum(e, axis=0, keepdims=True)
-        grad_probs = lax.dot_general(v, g, NT, preferred_element_type=F32)
         delta = jnp.sum(e * grad_probs, axis=0, keepdims=True) * inverse
         p = e * (inverse * factors[j] * scaling)
-        low = p.astype(BF16)
-        ds = (p * (grad_probs - delta)).astype(BF16)
+        return p.astype(BF16), (p * (grad_probs - delta)).astype(BF16)
+
+    def gradients(j, low, ds):
+        window, q, g, k, _ = operands(j)
         grad_query.append(lax.dot_general(ds, k, TN, preferred_element_type=F32).astype(BF16))
         grad_key[window] += jnp.dot(ds, q, preferred_element_type=F32)
         grad_value[window] += jnp.dot(low, g, preferred_element_type=F32)
+
+    first, second = {}, {}
+    for t in range(chunks + 2):
+        if t < chunks:
+            first[t] = products(t)
+        if 0 <= t - 2:
+            gradients(t - 2, *second.pop(t - 2))
+        if 0 <= t - 1 < chunks:
+            second[t - 1] = weights(t - 1, *first.pop(t - 1))
     return jnp.concatenate(grad_query, axis=0)
 
 
@@ -245,6 +260,17 @@
             cross_copy(n).wait_send()
 
 
+def write_kernel(gq, gk, gv, gq_hbm, gk_hbm, gv_hbm, sems):
+    copies = [
+        pltpu.make_async_copy(src, dst, sems.at[n])
+        for n, (src, dst) in enumerate(((gq, gq_hbm), (gk, gk_hbm), (gv, gv_hbm)))
+    ]
+    for copy in copies:
+        copy.start()
+    for copy in copies:
+        copy.wait()
+
+
 def per_device(shards, ranks, queries, keys, values, grad_out, exponents, lengths):
     tokens, groups, heads, width = queries.shape
     chunks = 4
@@ -260,7 +286,7 @@
     )
     pair = (2, tokens, width)
     dma = pltpu.SemaphoreType.DMA
-    return pl.pallas_call(
+    results = pl.pallas_call(
         functools.partial(fused_kernel, chunk, shards, ranks),
         grid=(groups,),
         in_specs=[smem, smem, rows_spec, rows_spec, vmem, vmem],
@@ -296,6 +322,13 @@
             collective_id=0, has_side_effects=True, vmem_limit_bytes=60 * 1024 * 1024
         ),
     )(lengths, levels, queries, grad_out, keys, values)
+    return pl.pallas_call(
+        write_kernel,
+        in_specs=[vmem] * 3,
+        out_specs=[pl.BlockSpec(memory_space=pltpu.HBM)] * 3,
+        out_shape=[jax.ShapeDtypeStruct(r.shape, r.dtype) for r in results],
+        scratch_shapes=[dma((3,))],
+    )(*results)
 
 
 def solution(mesh):

time: 34.7 us -> 40 us (1.15)
  Pallas kernels: 31 us -> 36.4 us
    pallas_call x0 -> x1, Pallas kernels: none -> 3.19 us  [per_device(): pl.pallas_call(write_kernel, in_specs=[vmem] * 3, out_specs=[pl.BlockSpec...]
    pallas_call x1, Pallas kernels: 31 us -> 33.2 us  [per_device(): pl.pallas_call(functools.partial(fused_kernel, chunk, shards, ranks), gri...]
    unnamed x3 -> x6, local copies, waits for them, and re-layouts: 2.73 us -> 2.74 us
where the time goes in v4:
time: 40 us; the launch traced here: 39.8 us
  Pallas kernels  36.4 us (91%)
  local copies, waits for them, and re-layouts  2.74 us (7%)
  between operations  0.65 us (2%)
    pallas_call x1, Pallas kernels, per_device(): pl.pallas_call(functools.partial(fused_kernel, chunk, shards, ranks), gri...  33.2 us
    pallas_call x1, Pallas kernels, per_device(): pl.pallas_call(write_kernel, in_specs=[vmem] * 3, out_specs=[pl.BlockSpec...  3.19 us
    unnamed x6, local copies, waits for them, and re-layouts  2.74 us

profile of v4, /device:TPU:1, one launch (start us, length us, event | category | flops | bytes accessed | tf_op | source)
XLA Modules:
  0.0 39.8 jit_solution(2005250848521019336)
XLA Ops:
  0.6 33.2 %shard_map.85 = (bf16[256,8,4,128]{3,2,1,0:T(4,128)(2,1)S(1)}, bf16[256,4,128]{2,1,0:T(4,128)(2,1)S(1)}, bf16[256,4,128]{2,1,0:T(4,128)(2,1)S(1)}) custom-call(s32[32]{0:T(128)} %lengths.1, s32[2,4,8]{2,1,0:T(4,128)} %bitcast.1, bf16[256,8,4,128]{3,2,1,0:T(4,128)(2,1)} %q_ref.1, bf16[256,8,4,128]{3,2,1,0:T(4,128)(2,1)} %go_ref.1, ...), custom_call_target="tpu_custom_call" | custom-call | tf_op jit(solution)/shard_map/pallas_call | solution.py:289
  33.9 0.0 copy-start
  33.9 1.3 %copy-done = bf16[256,8,4,128]{3,2,1,0:T(4,128)(2,1)} copy-done((bf16[256,8,4,128]{3,2,1,0:T(4,128)(2,1)}, bf16[256,8,4,128]{3,2,1,0:T(4,128)(2,1)S(1)}, u32[]{:S(2)}) %copy-start) | copy-done | bytes 2097176
  35.2 0.0 copy-start.1
  35.2 0.7 %copy-done.1 = bf16[256,4,128]{2,1,0:T(4,128)(2,1)} copy-done((bf16[256,4,128]{2,1,0:T(4,128)(2,1)}, bf16[256,4,128]{2,1,0:T(4,128)(2,1)S(1)}, u32[]{:S(2)}) %copy-start.1) | copy-done | bytes 262168
  35.9 0.0 copy-start.2
  35.9 0.7 %copy-done.2 = bf16[256,4,128]{2,1,0:T(4,128)(2,1)} copy-done((bf16[256,4,128]{2,1,0:T(4,128)(2,1)}, bf16[256,4,128]{2,1,0:T(4,128)(2,1)S(1)}, u32[]{:S(2)}) %copy-start.2) | copy-done | bytes 262168
  36.6 3.2 %shard_map.86 = (bf16[256,8,4,128]{3,2,1,0:T(4,128)(2,1)}, bf16[256,4,128]{2,1,0:T(4,128)(2,1)}, bf16[256,4,128]{2,1,0:T(4,128)(2,1)}) custom-call(bf16[256,8,4,128]{3,2,1,0:T(4,128)(2,1)} %copy-done, bf16[256,4,128]{2,1,0:T(4,128)(2,1)} %copy-done.1, bf16[256,4,128]{2,1,0:T(4,128)(2,1)} %copy-done.2), custom_call_target="tpu_custom_call" | custom-call | tf_op jit(solution)/shard_map/pallas_call | solution.py:325
Async XLA Ops:
  33.9 1.3 %copy-start = (bf16[256,8,4,128]{3,2,1,0:T(4,128)(2,1)}, bf16[256,8,4,128]{3,2,1,0:T(4,128)(2,1)S(1)}, u32[]{:S(2)}) copy-start(bf16[256,8,4,128]{3,2,1,0:T(4,128)(2,1)S(1)} %get-tuple-element.6.gq) | copy-start | bytes 6291460
  35.2 0.7 %copy-start.1 = (bf16[256,4,128]{2,1,0:T(4,128)(2,1)}, bf16[256,4,128]{2,1,0:T(4,128)(2,1)S(1)}, u32[]{:S(2)}) copy-start(bf16[256,4,128]{2,1,0:T(4,128)(2,1)S(1)} %get-tuple-element.7.gk) | copy-start | bytes 786436
  35.9 0.7 %copy-start.2 = (bf16[256,4,128]{2,1,0:T(4,128)(2,1)}, bf16[256,4,128]{2,1,0:T(4,128)(2,1)S(1)}, u32[]{:S(2)}) copy-start(bf16[256,4,128]{2,1,0:T(4,128)(2,1)S(1)} %get-tuple-element.8.gv) | copy-start | bytes 786436

commit v5 on v4

--- a/solution.py
+++ b/solution.py
@@ -12,8 +12,8 @@
 NT = (((1,), (1,)), ((), ()))
 TN = (((0,), (0,)), ((), ()))
 MESH = pl.DeviceIdType.MESH
-AHEAD = 3
-LAG = 2
+AHEAD = 2
+LAG = 3
 
 
 def fill_bias(bias, lengths, first, heads, chunk):
@@ -166,9 +166,8 @@
                     barrier, ranks - 1 + has_next.astype(jnp.int32) + has_prev.astype(jnp.int32)
                 )
                 send_window(0)
-        send_window(1)
         fill_bias(bias, lengths, shard * tokens, heads, chunk)
-        for n in range(2, AHEAD):
+        for n in range(1, AHEAD):
             send_window(n)
 
     @pl.when(i + AHEAD < groups)
@@ -258,17 +257,6 @@
 
         for n in range(foreign):
             cross_copy(n).wait_send()
-
-
-def write_kernel(gq, gk, gv, gq_hbm, gk_hbm, gv_hbm, sems):
-    copies = [
-        pltpu.make_async_copy(src, dst, sems.at[n])
-        for n, (src, dst) in enumerate(((gq, gq_hbm), (gk, gk_hbm), (gv, gv_hbm)))
-    ]
-    for copy in copies:
-        copy.start()
-    for copy in copies:
-        copy.wait()
 
 
 def per_device(shards, ranks, queries, keys, values, grad_out, exponents, lengths):
@@ -286,7 +274,7 @@
     )
     pair = (2, tokens, width)
     dma = pltpu.SemaphoreType.DMA
-    results = pl.pallas_call(
+    return pl.pallas_call(
         functools.partial(fused_kernel, chunk, shards, ranks),
         grid=(groups,),
         in_specs=[smem, smem, rows_spec, rows_spec, vmem, vmem],
@@ -322,13 +310,6 @@
             collective_id=0, has_side_effects=True, vmem_limit_bytes=60 * 1024 * 1024
         ),
     )(lengths, levels, queries, grad_out, keys, values)
-    return pl.pallas_call(
-        write_kernel,
-        in_specs=[vmem] * 3,
-        out_specs=[pl.BlockSpec(memory_space=pltpu.HBM)] * 3,
-        out_shape=[jax.ShapeDtypeStruct(r.shape, r.dtype) for r in results],
-        scratch_shapes=[dma((3,))],
-    )(*results)
 
 
 def solution(mesh):

time: 40 us -> 38.5 us (0.963)
  Pallas kernels: 36.4 us -> 34.9 us
    pallas_call x1 -> x0, Pallas kernels: 3.19 us -> none  [per_device(): pl.pallas_call(write_kernel, in_specs=[vmem] * 3, out_specs=[pl.BlockSpec...]
    pallas_call x1, Pallas kernels: 33.2 us -> 34.9 us  [per_device(): pl.pallas_call(functools.partial(fused_kernel, chunk, shards, ranks), gri...]
    unnamed x6 -> x3, local copies, waits for them, and re-layouts: 2.74 us -> 2.73 us
where the time goes in v5:
time: 38.5 us; the launch traced here: 38.3 us
  Pallas kernels  34.9 us (91%)
  local copies, waits for them, and re-layouts  2.73 us (7%)
  between operations  0.64 us (2%)
    pallas_call x1, Pallas kernels, per_device(): pl.pallas_call(functools.partial(fused_kernel, chunk, shards, ranks), gri...  34.9 us
    unnamed x3, local copies, waits for them, and re-layouts  2.73 us

profile of v5, /device:TPU:1, one launch (start us, length us, event | category | flops | bytes accessed | tf_op | source)
XLA Modules:
  0.0 38.3 jit_solution(10840178325519666922)
XLA Ops:
  0.6 34.9 %shard_map.85 = (bf16[256,8,4,128]{3,2,1,0:T(4,128)(2,1)S(1)}, bf16[256,4,128]{2,1,0:T(4,128)(2,1)S(1)}, bf16[256,4,128]{2,1,0:T(4,128)(2,1)S(1)}) custom-call(s32[32]{0:T(128)} %lengths.1, s32[2,4,8]{2,1,0:T(4,128)} %bitcast.1, bf16[256,8,4,128]{3,2,1,0:T(4,128)(2,1)} %q_ref.1, bf16[256,8,4,128]{3,2,1,0:T(4,128)(2,1)} %go_ref.1, ...), custom_call_target="tpu_custom_call" | custom-call | tf_op jit(solution)/shard_map/pallas_call | solution.py:277
  35.6 1.3 %copy.12 = bf16[256,8,4,128]{3,2,1,0:T(4,128)(2,1)} copy(bf16[256,8,4,128]{3,2,1,0:T(4,128)(2,1)S(1)} %get-tuple-element.3) | data formatting | bytes 4194304
  36.9 0.7 %copy.13 = bf16[256,4,128]{2,1,0:T(4,128)(2,1)} copy(bf16[256,4,128]{2,1,0:T(4,128)(2,1)S(1)} %get-tuple-element.4) | data formatting | bytes 524288
  37.6 0.7 %copy.14 = bf16[256,4,128]{2,1,0:T(4,128)(2,1)} copy(bf16[256,4,128]{2,1,0:T(4,128)(2,1)S(1)} %get-tuple-element.5) | data formatting | bytes 524288

commit v6 on v5

--- a/solution.py
+++ b/solution.py
@@ -12,7 +12,7 @@
 NT = (((1,), (1,)), ((), ()))
 TN = (((0,), (0,)), ((), ()))
 MESH = pl.DeviceIdType.MESH
-AHEAD = 2
+AHEAD = 4
 LAG = 3
 
 

time: 38.5 us -> 38.5 us (level)
  no operation moved by 1% of the time
where the time goes in v6:
time: 38.5 us; the launch traced here: 38.3 us
  Pallas kernels  34.9 us (91%)
  local copies, waits for them, and re-layouts  2.73 us (7%)
  between operations  0.64 us (2%)
    pallas_call x1, Pallas kernels, per_device(): pl.pallas_call(functools.partial(fused_kernel, chunk, shards, ranks), gri...  34.9 us
    unnamed x3, local copies, waits for them, and re-layouts  2.73 us

profile of v6, /device:TPU:1, one launch (start us, length us, event | category | flops | bytes accessed | tf_op | source)
XLA Modules:
  0.0 38.3 jit_solution(8729043921410444148)
XLA Ops:
  0.6 34.9 %shard_map.85 = (bf16[256,8,4,128]{3,2,1,0:T(4,128)(2,1)S(1)}, bf16[256,4,128]{2,1,0:T(4,128)(2,1)S(1)}, bf16[256,4,128]{2,1,0:T(4,128)(2,1)S(1)}) custom-call(s32[32]{0:T(128)} %lengths.1, s32[2,4,8]{2,1,0:T(4,128)} %bitcast.1, bf16[256,8,4,128]{3,2,1,0:T(4,128)(2,1)} %q_ref.1, bf16[256,8,4,128]{3,2,1,0:T(4,128)(2,1)} %go_ref.1, ...), custom_call_target="tpu_custom_call" | custom-call | tf_op jit(solution)/shard_map/pallas_call | solution.py:277
  35.6 1.3 %copy.12 = bf16[256,8,4,128]{3,2,1,0:T(4,128)(2,1)} copy(bf16[256,8,4,128]{3,2,1,0:T(4,128)(2,1)S(1)} %get-tuple-element.3) | data formatting | bytes 4194304
  36.9 0.7 %copy.13 = bf16[256,4,128]{2,1,0:T(4,128)(2,1)} copy(bf16[256,4,128]{2,1,0:T(4,128)(2,1)S(1)} %get-tuple-element.4) | data formatting | bytes 524288
  37.6 0.7 %copy.14 = bf16[256,4,128]{2,1,0:T(4,128)(2,1)} copy(bf16[256,4,128]{2,1,0:T(4,128)(2,1)S(1)} %get-tuple-element.5) | data formatting | bytes 524288
